TPU v7x, 256 devices: a whole 4x4x8 slice. The times are simulated.
256 devices in a mesh: gx: 8 (over z_hi, core), gy: 4 (over x), gz: 8 (over z_lo, y).
Axes of the slice: x: 4, y: 4, z: 8 (z_hi: 4, z_lo: 2; z = z_hi * 2 + z_lo), core: 2. Of those that a mesh axis runs over, the one named last changes fastest.
Arguments:
- tokens: bfloat16 [1024, 8192], P('gy', ('gz', 'gx')), may hold values from -6 to 6
- gate_weight: bfloat16 [8192, 14336], P('gz', ('gx', 'gy')), may hold values from -0.0625 to 0.0625
- up_weight: bfloat16 [8192, 14336], P('gz', ('gx', 'gy')), may hold values from -0.0625 to 0.0625
- down_weight: bfloat16 [14336, 8192], P('gx', ('gz', 'gy')), may hold values from -0.046875 to 0.046875
- out_grad: bfloat16 [1024, 8192], P('gy', ('gz', 'gx')), may hold values from -6 to 6
Outputs:
- mixed: bfloat16 [1024, 8192], P('gy', ('gz', 'gx'))
- tokens_grad: bfloat16 [1024, 8192], P('gy', ('gz', 'gx'))
- gate_grad: bfloat16 [8192, 14336], P('gz', ('gx', 'gy'))
- up_grad: bfloat16 [8192, 14336], P('gz', ('gx', 'gy'))
- down_grad: bfloat16 [14336, 8192], P('gx', ('gz', 'gy'))
All inputs are finite; a program needn't handle non-finite values.
Results may differ from a plain program's by a relative error of at most 0.0049.
Values may be sent and summed in bfloat16 or wider, within the bound.
No kernel may reach another device: no remote copies, remote signals or barrier semaphores. Data moves between devices by JAX's collectives and lax.ppermute only.
A program may use at most 128 MiB of HBM per device.

v0:
```python
import jax
import jax.numpy as jnp
from jax import lax
from jax.sharding import PartitionSpec as P


def matmul(left, right):
    return jnp.dot(left, right, preferred_element_type=jnp.float32)


def matmul_right_t(left, right):
    return lax.dot_general(
        left, right, (((1,), (1,)), ((), ())), preferred_element_type=jnp.float32
    )


def matmul_left_t(left, right):
    return lax.dot_general(
        left, right, (((0,), (0,)), ((), ())), preferred_element_type=jnp.float32
    )


def local(tokens, gate_weight, up_weight, down_weight, out_grad):
    tok_cols, grad_cols = (
        lax.all_gather(tokens, "gx", axis=1, tiled=True),
        lax.all_gather(out_grad, "gx", axis=1, tiled=True),
    )
    gate_full, up_full, down_full = (
        lax.all_gather(gate_weight, "gy", axis=1, tiled=True),
        lax.all_gather(up_weight, "gy", axis=1, tiled=True),
        lax.all_gather(down_weight, "gy", axis=1, tiled=True),
    )
    gate_part = matmul(tok_cols, gate_full)
    up_part = matmul(tok_cols, up_full)
    gate_rows, up_rows = (
        lax.psum_scatter(gate_part, "gz", scatter_dimension=0, tiled=True),
        lax.psum_scatter(up_part, "gz", scatter_dimension=0, tiled=True),
    )
    sig = jax.nn.sigmoid(gate_rows)
    act = gate_rows * sig
    hidden = (act * up_rows).astype(jnp.bfloat16)
    hidden_all = lax.all_gather(hidden, "gz", axis=0, tiled=True)
    out_part = matmul(hidden_all, down_full)
    mixed = lax.psum_scatter(out_part, "gx", scatter_dimension=1, tiled=True).astype(jnp.bfloat16)
    dh_part = matmul_right_t(grad_cols, down_full)
    dh_rows = lax.psum_scatter(dh_part, "gz", scatter_dimension=0, tiled=True)
    gate_delta = (dh_rows * up_rows * sig * (1.0 + gate_rows * (1.0 - sig))).astype(jnp.bfloat16)
    up_delta = (dh_rows * act).astype(jnp.bfloat16)
    gate_all, up_all = (
        lax.all_gather(gate_delta, "gz", axis=0, tiled=True),
        lax.all_gather(up_delta, "gz", axis=0, tiled=True),
    )
    dx_part = matmul_right_t(gate_all, gate_full) + matmul_right_t(up_all, up_full)
    tokens_grad = lax.psum_scatter(dx_part, "gx", scatter_dimension=1, tiled=True).astype(
        jnp.bfloat16
    )
    delta_gate, delta_up, grad_slice = (
        lax.all_to_all(gate_all, "gy", split_axis=1, concat_axis=0, tiled=True),
        lax.all_to_all(up_all, "gy", split_axis=1, concat_axis=0, tiled=True),
        lax.all_to_all(grad_cols, "gy", split_axis=1, concat_axis=0, tiled=True),
    )
    pieces = (
        lax.all_gather(tok_cols, "gy", axis=0, tiled=True),
        lax.all_gather(hidden_all, "gy", axis=0, tiled=True),
    )
    gate_grad = matmul_left_t(pieces[0], delta_gate)
    up_grad = matmul_left_t(pieces[0], delta_up)
    down_grad = matmul_left_t(pieces[1], grad_slice)
    return (
        mixed,
        tokens_grad,
        gate_grad.astype(jnp.bfloat16),
        up_grad.astype(jnp.bfloat16),
        down_grad.astype(jnp.bfloat16),
    )


def solution(mesh):
    in_specs = (
        P("gy", ("gz", "gx")),
        P("gz", ("gx", "gy")),
        P("gz", ("gx", "gy")),
        P("gx", ("gz", "gy")),
        P("gy", ("gz", "gx")),
    )
    out_specs = (
        P("gy", ("gz", "gx")),
        P("gy", ("gz", "gx")),
        P("gz", ("gx", "gy")),
        P("gz", ("gx", "gy")),
        P("gx", ("gz", "gy")),
    )
    return jax.shard_map(local, mesh=mesh, in_specs=in_specs, out_specs=out_specs, check_vma=False)
```

profile of v0, /device:TPU:1, one launch (start us, length us, event | category | flops | bytes accessed | tf_op | source)
XLA Modules:
  0.0 502.1 jit_solution(10327820006403604461)
XLA Ops:
  7.2 0.7 all-gather.6.cloned.1.call-update
  7.9 0.7 all-gather.8.cloned.1.call-update
  8.7 0.7 all-gather.10.cloned.1.call-update
  9.4 0.0 reduce-scatter.6.cloned.1.call-start
  9.4 22.2 %all_gather.30 = bf16[256,1024]{1,0:T(8,128)(2,1)S(1)} all-gather(bf16[256,128]{1,0:T(8,128)(2,1)} %param.5), channel_id=1, replica_groups=mesh['gx'=8,'gy'=4,'gz'=8] {'gx'}, dimensions={1}, use_global_device_ids=true | all-gather | bytes 589824 | tf_op jit(solution)/shard_map/all_gather | solution.py:25
  31.6 28.5 %all-gather.6.cloned.1.call-done = bf16[1024,1792]{0,1:T(8,128)(2,1)} async-done(((bf16[1024,448]{0,1:T(8,128)(2,1)}), bf16[1024,1792]{0,1:T(8,128)(2,1)}) %all-gather.6.cloned.1.call-update) | async-done | bytes 3670032 | tf_op jit(solution)/shard_map/all_gather | solution.py:29
  60.1 4.4 fusion.3
  64.5 0.0 reduce-scatter.8.cloned.1.call-start
  64.6 44.1 %all-gather.8.cloned.1.call-done = bf16[1024,1792]{0,1:T(8,128)(2,1)} async-done(((bf16[1024,448]{0,1:T(8,128)(2,1)}), bf16[1024,1792]{0,1:T(8,128)(2,1)}) %all-gather.8.cloned.1.call-update) | async-done | bytes 3670032 | tf_op jit(solution)/shard_map/all_gather | solution.py:30
  108.7 4.4 fusion.4
  113.1 0.0 reduce-scatter.12.cloned.1.call-start
  113.2 0.1 copy.14
  113.3 19.1 %all_gather.35 = bf16[256,1024]{0,1:T(8,128)(2,1)} all-gather(bf16[256,128]{0,1:T(8,128)(2,1)S(1)} %copy.14), channel_id=1, replica_groups=mesh['gx'=8,'gy'=4,'gz'=8] {'gx'}, dimensions={1}, use_global_device_ids=true | all-gather | bytes 589824 | tf_op jit(solution)/shard_map/all_gather | solution.py:26
  132.4 27.6 %all-gather.10.cloned.1.call-done = bf16[1792,1024]{1,0:T(8,128)(2,1)} async-done(((bf16[1792,256]{1,0:T(8,128)(2,1)}), bf16[1792,1024]{1,0:T(8,128)(2,1)}) %all-gather.10.cloned.1.call-update) | async-done | bytes 3670032 | tf_op jit(solution)/shard_map/all_gather | solution.py:31
  160.0 4.6 fusion.6
  164.7 0.0 all-gather.12.cloned.1.call-start
  164.7 0.7 all-gather.12.cloned.1.call-update
  165.5 37.9 %reduce-scatter.6.cloned.1.call-done = f32[32,1792]{1,0:T(8,128)} async-done(((f32[256,1792]{1,0:T(8,128)}), f32[32,1792]{1,0:T(8,128)}) %reduce-scatter.6.cloned.1.call-update) | async-done | bytes 229392 | tf_op jit(solution)/shard_map/reduce_scatter | solution.py:36
  203.3 45.6 %reduce-scatter.8.cloned.1.call-done = f32[32,1792]{1,0:T(8,128)} async-done(((f32[256,1792]{1,0:T(8,128)}), f32[32,1792]{1,0:T(8,128)}) %reduce-scatter.8.cloned.1.call-update) | async-done | bytes 229392 | tf_op jit(solution)/shard_map/reduce_scatter | solution.py:37
  248.9 45.7 %reduce-scatter.12.cloned.1.call-done = f32[32,1792]{1,0:T(8,128)} async-done(((f32[256,1792]{1,0:T(8,128)}), f32[32,1792]{1,0:T(8,128)}) %reduce-scatter.12.cloned.1.call-update) | async-done | bytes 229392 | tf_op jit(solution)/shard_map/reduce_scatter | solution.py:46
  294.6 1.3 multiply_convert_fusion
  295.9 23.4 %all_gather.36 = bf16[256,1792]{1,0:T(8,128)(2,1)S(1)} all-gather(bf16[32,1792]{1,0:T(8,128)(2,1)S(1)} %get-tuple-element.6), channel_id=1, replica_groups=mesh['gx'=8,'gy'=4,'gz'=8] {'gz'}, dimensions={0}, use_global_device_ids=true | all-gather | bytes 1032192 | tf_op jit(solution)/shard_map/all_gather | solution.py:50
  319.3 3.3 fusion.7
  322.6 24.5 %all_gather.37 = bf16[256,1792]{1,0:T(8,128)(2,1)S(1)} all-gather(bf16[32,1792]{1,0:T(8,128)(2,1)S(1)} %get-tuple-element.5), channel_id=1, replica_groups=mesh['gx'=8,'gy'=4,'gz'=8] {'gz'}, dimensions={0}, use_global_device_ids=true | all-gather | bytes 1032192 | tf_op jit(solution)/shard_map/all_gather | solution.py:51
  347.1 2.1 convolution_add_fusion
  349.3 0.0 reduce-scatter.10.cloned.1.call-start
  349.3 23.8 %all_gather.33 = bf16[256,1792]{1,0:T(8,128)(2,1)S(1)} all-gather(bf16[32,1792]{1,0:T(8,128)(2,1)S(1)} %get-tuple-element.7), channel_id=1, replica_groups=mesh['gx'=8,'gy'=4,'gz'=8] {'gz'}, dimensions={0}, use_global_device_ids=true | all-gather | bytes 1032192 | tf_op jit(solution)/shard_map/all_gather | solution.py:42
  373.1 4.5 fusion.5
  377.6 0.0 all-gather.14.cloned.1.call-start
  377.6 0.5 all-gather.14.cloned.1.call-update
  378.2 4.6 all-to-all-start.2
  382.8 1.3 copy.15
  384.1 5.9 %all-to-all-done.2 = bf16[256,4,256]{0,2,1:T(8,128)(2,1)S(1)} async-done(((bf16[256,4,256]{0,2,1:T(8,128)(2,1)}), bf16[256,4,256]{0,2,1:T(8,128)(2,1)S(1)}, u32[]{:S(2)}, u32[]{:S(2)}) %all-to-all-start.2) | async-done | bytes 524320 | tf_op jit(solution)/shard_map/all_to_all | solution.py:60
  390.0 3.5 all-to-all-start
  393.6 1.3 copy.17
  394.8 8.1 %all-to-all-done = bf16[256,4,448]{0,2,1:T(8,128)(2,1)S(1)} async-done(((bf16[256,4,448]{0,2,1:T(8,128)(2,1)}), bf16[256,4,448]{0,2,1:T(8,128)(2,1)S(1)}, u32[]{:S(2)}, u32[]{:S(2)}) %all-to-all-start) | async-done | bytes 917536 | tf_op jit(solution)/shard_map/all_to_all | solution.py:58
  402.9 3.7 all-to-all-start.1
  406.6 0.2 copy.19
  406.8 0.1 copy.20
  406.9 11.3 %all-to-all-done.1 = bf16[256,4,448]{0,2,1:T(8,128)(2,1)S(1)} async-done(((bf16[256,4,448]{0,2,1:T(8,128)(2,1)}), bf16[256,4,448]{0,2,1:T(8,128)(2,1)S(1)}, u32[]{:S(2)}, u32[]{:S(2)}) %all-to-all-start.1) | async-done | bytes 917536 | tf_op jit(solution)/shard_map/all_to_all | solution.py:59
  418.2 0.1 copy.21
  418.4 3.8 fusion
  422.2 2.1 fusion.1
  424.2 1.5 convert_element_type.34
  425.8 17.7 %reduce-scatter.10.cloned.1.call-done = f32[256,128]{1,0:T(8,128)} async-done(((f32[256,1024]{1,0:T(8,128)}), f32[256,128]{1,0:T(8,128)}) %reduce-scatter.10.cloned.1.call-update) | async-done | bytes 131088 | tf_op jit(solution)/shard_map/reduce_scatter | solution.py:44
  443.5 1.5 convert_element_type.31
  445.1 46.1 %all-gather.14.cloned.1.call-done = bf16[1024,1792]{1,0:T(8,128)(2,1)} async-done(((bf16[256,1792]{1,0:T(8,128)(2,1)}), bf16[1024,1792]{1,0:T(8,128)(2,1)}) %all-gather.14.cloned.1.call-update) | async-done | bytes 3670032 | tf_op jit(solution)/shard_map/all_gather | solution.py:64
  491.2 4.1 convolution_convert_fusion
  (21 shorter events, 0.3 us)
Async XLA Ops:
  7.2 52.9 %all-gather.6.cloned.1.call-start = ((), (), s32[]{:S(2)}) async-start(), calls=%async_computation.8 | async-start | bytes 4587520 | tf_op jit(solution)/shard_map/all_gather | solution.py:29
  7.9 100.8 %all-gather.8.cloned.1.call-start = ((), (), s32[]{:S(2)}) async-start(), calls=%async_computation.10 | async-start | bytes 4587520 | tf_op jit(solution)/shard_map/all_gather | solution.py:30
  8.6 151.4 %all-gather.10.cloned.1.call-start = ((), (), s32[]{:S(2)}) async-start(), calls=%async_computation.12 | async-start | bytes 4587520 | tf_op jit(solution)/shard_map/all_gather | solution.py:31
  9.4 193.9 %reduce-scatter.6.cloned.1.call-start = ((), (), s32[]{:S(2)}) async-start(), calls=%async_computation.9 | async-start | bytes 2064384 | tf_op jit(solution)/shard_map/reduce_scatter | solution.py:36
  31.6 77.1 %copy-start.1 = (bf16[256,1024]{1,0:T(8,128)(2,1)}, bf16[256,1024]{1,0:T(8,128)(2,1)S(1)}, u32[]{:S(2)}) copy-start(bf16[256,1024]{1,0:T(8,128)(2,1)S(1)} %all_gather.30) | copy-start | bytes 1572868
  64.5 48.7 %copy-start.2 = (bf16[256,128]{1,0:T(8,128)(2,1)S(1)}, bf16[256,128]{1,0:T(8,128)(2,1)}, u32[]{:S(2)}) copy-start(bf16[256,128]{1,0:T(8,128)(2,1)} %param.9) | copy-start | bytes 196612
  64.5 184.4 %reduce-scatter.8.cloned.1.call-start = ((), (), s32[]{:S(2)}) async-start(), calls=%async_computation.11 | async-start | bytes 2064384 | tf_op jit(solution)/shard_map/reduce_scatter | solution.py:37
  113.1 181.4 %reduce-scatter.12.cloned.1.call-start = ((), (), s32[]{:S(2)}) async-start(), calls=%async_computation.14 | async-start | bytes 2064384 | tf_op jit(solution)/shard_map/reduce_scatter | solution.py:46
  164.7 253.7 %all-gather.12.cloned.1.call-start = ((), (), s32[]{:S(2)}) async-start(), calls=%async_computation.16 | async-start | bytes 2621440 | tf_op jit(solution)/shard_map/all_gather | solution.py:63
  165.4 258.8 %reduce-scatter.14.cloned.1.call-start = ((), (), s32[]{:S(2)}) async-start(), calls=%async_computation.15 | async-start | bytes 1179648 | tf_op jit(solution)/shard_map/reduce_scatter | solution.py:54
  319.3 27.9 %copy-start.3 = (bf16[1024,1792]{0,1:T(8,128)(2,1)S(1)}, bf16[1024,1792]{0,1:T(8,128)(2,1)}, u32[]{:S(2)}) copy-start(bf16[1024,1792]{0,1:T(8,128)(2,1)} %all-gather.8.cloned.1.call-done) | copy-start | bytes 11010052
  349.3 94.3 %reduce-scatter.10.cloned.1.call-start = ((), (), s32[]{:S(2)}) async-start(), calls=%async_computation.13 | async-start | bytes 1179648 | tf_op jit(solution)/shard_map/reduce_scatter | solution.py:44
  373.1 4.5 copy-start
  377.6 113.6 %all-gather.14.cloned.1.call-start = ((), (), s32[]{:S(2)}) async-start(), calls=%async_computation.17 | async-start | bytes 4587520 | tf_op jit(solution)/shard_map/all_gather | solution.py:64
  378.2 11.9 %all-to-all-start.2 = ((bf16[256,4,256]{0,2,1:T(8,128)(2,1)}), bf16[256,4,256]{0,2,1:T(8,128)(2,1)S(1)}, u32[]{:S(2)}, u32[]{:S(2)}) async-start(bf16[256,4,256]{0,2,1:T(8,128)(2,1)} %bitcast.6), calls=%async_computation.7 | async-start | bytes 1048576 | tf_op jit(solution)/shard_map/all_to_all | solution.py:60
  390.0 12.9 %all-to-all-start = ((bf16[256,4,448]{0,2,1:T(8,128)(2,1)}), bf16[256,4,448]{0,2,1:T(8,128)(2,1)S(1)}, u32[]{:S(2)}, u32[]{:S(2)}) async-start(bf16[256,4,448]{0,2,1:T(8,128)(2,1)} %bitcast), calls=%async_computation.5 | async-start | bytes 1835008 | tf_op jit(solution)/shard_map/all_to_all | solution.py:58
  402.9 15.3 %all-to-all-start.1 = ((bf16[256,4,448]{0,2,1:T(8,128)(2,1)}), bf16[256,4,448]{0,2,1:T(8,128)(2,1)S(1)}, u32[]{:S(2)}, u32[]{:S(2)}) async-start(bf16[256,4,448]{0,2,1:T(8,128)(2,1)} %bitcast.3), calls=%async_computation.6 | async-start | bytes 1835008 | tf_op jit(solution)/shard_map/all_to_all | solution.py:59
  418.4 3.8 copy-start.4
Sparse Core Ops, SparseCore 0:
  9.8 50.2 all-gather.5
  61.9 46.7 all-gather.7
  110.5 49.5 all-gather.9
  162.4 40.8 reduce-scatter.5
  205.7 43.1 reduce-scatter.7
  251.3 43.1 reduce-scatter.11
  296.9 37.5 all-gather.11
  349.4 54.7 reduce-scatter.13
  406.8 36.7 reduce-scatter.9
  445.2 45.9 all-gather.13
where the time goes:
time: 503 us; the launch traced here: 502 us
  waiting for transfers between devices  322 us (64%)
  blocking collectives  113 us (22%)
  matrix products  33.4 us (7%)
  between operations  14.3 us (3%)
  starting transfers between devices  12.2 us (2%)
    all_gather x1, waiting for transfers between devices, local(): lax.all_gather(hidden_all, 'gy', axis=0, tiled=True)  46.1 us
    reduce_scatter x1, waiting for transfers between devices, local(): dh_rows = lax.psum_scatter(dh_part, 'gz', scatter_dimension=0, tiled=True)  45.7 us
    reduce_scatter x1, waiting for transfers between devices, local(): lax.psum_scatter(up_part, 'gz', scatter_dimension=0, tiled=True)  45.6 us
    all_gather x1, waiting for transfers between devices, local(): lax.all_gather(up_weight, 'gy', axis=1, tiled=True)  44.1 us
    reduce_scatter x1, waiting for transfers between devices, local(): lax.psum_scatter(gate_part, 'gz', scatter_dimension=0, tiled=True)  37.9 us
    all_gather x1, waiting for transfers between devices, local(): lax.all_gather(gate_weight, 'gy', axis=1, tiled=True)  28.5 us
    all_gather x1, waiting for transfers between devices, local(): lax.all_gather(down_weight, 'gy', axis=1, tiled=True)  27.6 us
    all_gather x1, blocking collectives, local(): lax.all_gather(up_delta, 'gz', axis=0, tiled=True)  24.5 us
  transfers between devices with their start and end apart: 13, of which 11 were waited for; matrix products, arithmetic and copies ran while one was open for 7% of the time, Pallas kernels for 0%

commit v1 on v0

--- a/solution.py
+++ b/solution.py
@@ -47,7 +47,9 @@
     gate_delta = (dh_rows * up_rows * sig * (1.0 + gate_rows * (1.0 - sig))).astype(jnp.bfloat16)
     up_delta = (dh_rows * act).astype(jnp.bfloat16)
     gate_all, up_all = (
-        lax.all_gather(gate_delta, "gz", axis=0, tiled=True),
+        jnp.concatenate(
+            lax.all_to_all(jnp.stack([gate_delta] * lax.axis_size("gz")), "gz", 0, 0), axis=0
+        ),
         lax.all_gather(up_delta, "gz", axis=0, tiled=True),
     )
     dx_part = matmul_right_t(gate_all, gate_full) + matmul_right_t(up_all, up_full)

time: 503 us -> 483 us (0.960)
  blocking collectives: 113 us -> 96.4 us
  waiting for transfers between devices: 322 us -> 310 us
    all_gather x1 -> x0, blocking collectives: 23.4 us -> none  [local(): lax.all_gather(gate_delta, 'gz', axis=0, tiled=True)]
    reduce_scatter x1, waiting for transfers between devices: 17.7 us -> 0.01 us  [local(): lax.psum_scatter(out_part, 'gx', scatter_dimension=1, tiled=True)]
    reduce_scatter x1, waiting for transfers between devices: 0.01 us -> 15.8 us  [local(): lax.psum_scatter(dx_part, 'gx', scatter_dimension=1, tiled=True)]
    all_gather x1, blocking collectives: 23.8 us -> 30.2 us  [local(): hidden_all = lax.all_gather(hidden, 'gz', axis=0, tiled=True)]
    all_to_all x1, waiting for transfers between devices: 8.07 us -> 2.83 us  [local(): lax.all_to_all(gate_all, 'gy', split_axis=1, concat_axis=0, tiled=True)]
    all_to_all x1, waiting for transfers between devices: 11.3 us -> 6.2 us  [local(): lax.all_to_all(up_all, 'gy', split_axis=1, concat_axis=0, tiled=True)]
  transfers between devices with their start and end apart: 13 -> 14, of which waited for: 11 -> 11; matrix products, arithmetic and copies ran while one was open for 7% -> 8% of each run, Pallas kernels for 0% -> 0%
where the time goes in v1:
time: 483 us; the launch traced here: 482 us
  waiting for transfers between devices  310 us (64%)
  blocking collectives  96.4 us (20%)
  matrix products  35.2 us (7%)
  starting transfers between devices  15.9 us (3%)
  between operations  14.3 us (3%)
  local copies, waits for them, and re-layouts  6.43 us (1%)
    all_gather x1, waiting for transfers between devices, local(): lax.all_gather(hidden_all, 'gy', axis=0, tiled=True)  46.2 us
    reduce_scatter x1, waiting for transfers between devices, local(): dh_rows = lax.psum_scatter(dh_part, 'gz', scatter_dimension=0, tiled=True)  45.7 us
    reduce_scatter x1, waiting for transfers between devices, local(): lax.psum_scatter(up_part, 'gz', scatter_dimension=0, tiled=True)  45.6 us
    all_gather x1, waiting for transfers between devices, local(): lax.all_gather(up_weight, 'gy', axis=1, tiled=True)  44.1 us
    reduce_scatter x1, waiting for transfers between devices, local(): lax.psum_scatter(gate_part, 'gz', scatter_dimension=0, tiled=True)  37.9 us
    all_gather x1, blocking collectives, local(): hidden_all = lax.all_gather(hidden, 'gz', axis=0, tiled=True)  30.2 us
    all_gather x1, waiting for transfers between devices, local(): lax.all_gather(gate_weight, 'gy', axis=1, tiled=True)  28.5 us
    all_gather x1, waiting for transfers between devices, local(): lax.all_gather(down_weight, 'gy', axis=1, tiled=True)  27.6 us
  transfers between devices with their start and end apart: 14, of which 11 were waited for; matrix products, arithmetic and copies ran while one was open for 8% of the time, Pallas kernels for 0%

profile of v1, /device:TPU:1, one launch (start us, length us, event | category | flops | bytes accessed | tf_op | source)
XLA Modules:
  0.0 482.2 jit_solution(6025222181400873222)
XLA Ops:
  7.2 0.7 all-gather.6.cloned.1.call-update
  7.9 0.7 all-gather.8.cloned.1.call-update
  8.7 0.7 all-gather.10.cloned.1.call-update
  9.4 22.2 %all_gather.27 = bf16[256,1024]{1,0:T(8,128)(2,1)S(1)} all-gather(bf16[256,128]{1,0:T(8,128)(2,1)} %param.5), channel_id=1, replica_groups=mesh['gx'=8,'gy'=4,'gz'=8] {'gx'}, dimensions={1}, use_global_device_ids=true | all-gather | bytes 589824 | tf_op jit(solution)/shard_map/all_gather | solution.py:25
  31.6 28.5 %all-gather.6.cloned.1.call-done = bf16[1024,1792]{0,1:T(8,128)(2,1)} async-done(((bf16[1024,448]{0,1:T(8,128)(2,1)}), bf16[1024,1792]{0,1:T(8,128)(2,1)}) %all-gather.6.cloned.1.call-update) | async-done | bytes 3670032 | tf_op jit(solution)/shard_map/all_gather | solution.py:29
  60.1 4.4 fusion.3
  64.5 0.0 reduce-scatter.8.cloned.1.call-start
  64.6 44.1 %all-gather.8.cloned.1.call-done = bf16[1024,1792]{0,1:T(8,128)(2,1)} async-done(((bf16[1024,448]{0,1:T(8,128)(2,1)}), bf16[1024,1792]{0,1:T(8,128)(2,1)}) %all-gather.8.cloned.1.call-update) | async-done | bytes 3670032 | tf_op jit(solution)/shard_map/all_gather | solution.py:30
  108.7 4.4 fusion.4
  113.1 0.0 reduce-scatter.12.cloned.1.call-start
  113.2 0.1 copy.18
  113.3 19.1 %all_gather.32 = bf16[256,1024]{0,1:T(8,128)(2,1)} all-gather(bf16[256,128]{0,1:T(8,128)(2,1)S(1)} %copy.18), channel_id=1, replica_groups=mesh['gx'=8,'gy'=4,'gz'=8] {'gx'}, dimensions={1}, use_global_device_ids=true | all-gather | bytes 589824 | tf_op jit(solution)/shard_map/all_gather | solution.py:26
  132.4 27.6 %all-gather.10.cloned.1.call-done = bf16[1792,1024]{1,0:T(8,128)(2,1)} async-done(((bf16[1792,256]{1,0:T(8,128)(2,1)}), bf16[1792,1024]{1,0:T(8,128)(2,1)}) %all-gather.10.cloned.1.call-update) | async-done | bytes 3670032 | tf_op jit(solution)/shard_map/all_gather | solution.py:31
  160.0 4.6 fusion.6
  164.7 0.0 all-gather.12.cloned.1.call-start
  164.7 0.7 all-gather.12.cloned.1.call-update
  165.4 37.9 %reduce-scatter.6.cloned.1.call-done = f32[32,1792]{1,0:T(8,128)} async-done(((f32[256,1792]{1,0:T(8,128)}), f32[32,1792]{1,0:T(8,128)}) %reduce-scatter.6.cloned.1.call-update) | async-done | bytes 229392 | tf_op jit(solution)/shard_map/reduce_scatter | solution.py:36
  203.3 45.6 %reduce-scatter.8.cloned.1.call-done = f32[32,1792]{1,0:T(8,128)} async-done(((f32[256,1792]{1,0:T(8,128)}), f32[32,1792]{1,0:T(8,128)}) %reduce-scatter.8.cloned.1.call-update) | async-done | bytes 229392 | tf_op jit(solution)/shard_map/reduce_scatter | solution.py:37
  248.9 45.7 %reduce-scatter.12.cloned.1.call-done = f32[32,1792]{1,0:T(8,128)} async-done(((f32[256,1792]{1,0:T(8,128)}), f32[32,1792]{1,0:T(8,128)}) %reduce-scatter.12.cloned.1.call-update) | async-done | bytes 229392 | tf_op jit(solution)/shard_map/reduce_scatter | solution.py:46
  294.6 1.3 multiply_convert_fusion
  295.9 1.0 stack.2
  296.8 4.1 all-to-all-start
  300.9 30.2 %all_gather.30 = bf16[256,1792]{1,0:T(8,128)(2,1)S(1)} all-gather(bf16[32,1792]{1,0:T(8,128)(2,1)S(1)} %get-tuple-element.7), channel_id=1, replica_groups=mesh['gx'=8,'gy'=4,'gz'=8] {'gz'}, dimensions={0}, use_global_device_ids=true | all-gather | bytes 1032192 | tf_op jit(solution)/shard_map/all_gather | solution.py:42
  331.2 4.5 fusion.5
  335.7 0.0 reduce-scatter.14.cloned.1.call-start
  335.7 25.0 %all_gather.33 = bf16[256,1792]{1,0:T(8,128)(2,1)S(1)} all-gather(bf16[32,1792]{1,0:T(8,128)(2,1)S(1)} %get-tuple-element.5), channel_id=1, replica_groups=mesh['gx'=8,'gy'=4,'gz'=8] {'gz'}, dimensions={0}, use_global_device_ids=true | all-gather | bytes 1032192 | tf_op jit(solution)/shard_map/all_gather | solution.py:53
  360.7 3.5 fusion.7
  364.2 2.1 convolution_add_fusion
  366.4 0.5 all-gather.14.cloned.1.call-update
  367.0 4.2 all-to-all-start.3
  371.2 1.3 copy.21
  372.5 5.9 %all-to-all-done.3 = bf16[256,4,256]{0,2,1:T(8,128)(2,1)S(1)} async-done(((bf16[256,4,256]{0,2,1:T(8,128)(2,1)}), bf16[256,4,256]{0,2,1:T(8,128)(2,1)S(1)}, u32[]{:S(2)}, u32[]{:S(2)}) %all-to-all-start.3) | async-done | bytes 524320 | tf_op jit(solution)/shard_map/all_to_all | solution.py:62
  378.4 3.5 all-to-all-start.2
  381.9 1.1 all_to_all.46
  383.0 1.7 copy.19
  384.7 6.2 %all-to-all-done.2 = bf16[256,4,448]{0,2,1:T(8,128)(2,1)S(1)} async-done(((bf16[256,4,448]{0,2,1:T(8,128)(2,1)}), bf16[256,4,448]{0,2,1:T(8,128)(2,1)S(1)}, u32[]{:S(2)}, u32[]{:S(2)}) %all-to-all-start.2) | async-done | bytes 917536 | tf_op jit(solution)/shard_map/all_to_all | solution.py:61
  390.9 3.7 all-to-all-start.1
  394.6 1.0 copy.23
  395.6 0.1 copy.25
  395.8 3.7 fusion.1
  399.5 1.5 convert_element_type.31
  401.0 2.8 all-to-all-done.1
  403.9 0.1 copy.24
  404.0 3.7 fusion
  407.7 15.8 %reduce-scatter.14.cloned.1.call-done = f32[256,128]{1,0:T(8,128)} async-done(((f32[256,1024]{1,0:T(8,128)}), f32[256,128]{1,0:T(8,128)}) %reduce-scatter.14.cloned.1.call-update) | async-done | bytes 131088 | tf_op jit(solution)/shard_map/reduce_scatter | solution.py:56
  423.5 1.5 convert_element_type.34
  425.1 46.2 %all-gather.14.cloned.1.call-done = bf16[1024,1792]{1,0:T(8,128)(2,1)} async-done(((bf16[256,1792]{1,0:T(8,128)(2,1)}), bf16[1024,1792]{1,0:T(8,128)(2,1)}) %all-gather.14.cloned.1.call-update) | async-done | bytes 3670032 | tf_op jit(solution)/shard_map/all_gather | solution.py:66
  471.3 4.1 convolution_convert_fusion
  (28 shorter events, 0.4 us)
Async XLA Ops:
  7.2 52.9 %all-gather.6.cloned.1.call-start = ((), (), s32[]{:S(2)}) async-start(), calls=%async_computation.9 | async-start | bytes 4587520 | tf_op jit(solution)/shard_map/all_gather | solution.py:29
  7.9 100.8 %all-gather.8.cloned.1.call-start = ((), (), s32[]{:S(2)}) async-start(), calls=%async_computation.11 | async-start | bytes 4587520 | tf_op jit(solution)/shard_map/all_gather | solution.py:30
  8.6 151.4 %all-gather.10.cloned.1.call-start = ((), (), s32[]{:S(2)}) async-start(), calls=%async_computation.13 | async-start | bytes 4587520 | tf_op jit(solution)/shard_map/all_gather | solution.py:31
  9.4 193.9 %reduce-scatter.6.cloned.1.call-start = ((), (), s32[]{:S(2)}) async-start(), calls=%async_computation.10 | async-start | bytes 2064384 | tf_op jit(solution)/shard_map/reduce_scatter | solution.py:36
  31.6 77.1 %copy-start.3 = (bf16[256,1024]{1,0:T(8,128)(2,1)}, bf16[256,1024]{1,0:T(8,128)(2,1)S(1)}, u32[]{:S(2)}) copy-start(bf16[256,1024]{1,0:T(8,128)(2,1)S(1)} %all_gather.27) | copy-start | bytes 1572868
  64.5 48.7 %copy-start.5 = (bf16[256,128]{1,0:T(8,128)(2,1)S(1)}, bf16[256,128]{1,0:T(8,128)(2,1)}, u32[]{:S(2)}) copy-start(bf16[256,128]{1,0:T(8,128)(2,1)} %param.9) | copy-start | bytes 196612
  64.5 184.4 %reduce-scatter.8.cloned.1.call-start = ((), (), s32[]{:S(2)}) async-start(), calls=%async_computation.12 | async-start | bytes 2064384 | tf_op jit(solution)/shard_map/reduce_scatter | solution.py:37
  113.1 181.4 %reduce-scatter.12.cloned.1.call-start = ((), (), s32[]{:S(2)}) async-start(), calls=%async_computation.15 | async-start | bytes 2064384 | tf_op jit(solution)/shard_map/reduce_scatter | solution.py:46
  164.7 231.1 %all-gather.12.cloned.1.call-start = ((), (), s32[]{:S(2)}) async-start(), calls=%async_computation.17 | async-start | bytes 2621440 | tf_op jit(solution)/shard_map/all_gather | solution.py:65
  296.8 63.8 %all-to-all-start = ((bf16[8,32,1792]{2,1,0:T(8,128)(2,1)}), bf16[8,32,1792]{2,1,0:T(8,128)(2,1)S(1)}, u32[]{:S(2)}, u32[]{:S(2)}) async-start(bf16[8,32,1792]{2,1,0:T(8,128)(2,1)} %stack.2), calls=%async_computation.4 | async-start | bytes 1835008 | tf_op jit(solution)/shard_map/all_to_all | solution.py:51
  300.9 98.6 %reduce-scatter.10.cloned.1.call-start = ((), (), s32[]{:S(2)}) async-start(), calls=%async_computation.14 | async-start | bytes 1179648 | tf_op jit(solution)/shard_map/reduce_scatter | solution.py:44
  331.2 4.5 copy-start
  335.7 87.9 %reduce-scatter.14.cloned.1.call-start = ((), (), s32[]{:S(2)}) async-start(), calls=%async_computation.16 | async-start | bytes 1179648 | tf_op jit(solution)/shard_map/reduce_scatter | solution.py:56
  360.7 5.7 %copy-start.1 = (bf16[8,32,1792]{2,1,0:T(8,128)(2,1)}, bf16[8,32,1792]{2,1,0:T(8,128)(2,1)S(1)}, u32[]{:S(2)}) copy-start(bf16[8,32,1792]{2,1,0:T(8,128)(2,1)S(1)} %all-to-all-done) | copy-start | bytes 2752516
  360.7 3.5 copy-start.6
  366.4 15.6 %copy-start.2 = (bf16[8,32,1792]{2,1,0:T(8,128)(2,1)S(1)}, bf16[8,32,1792]{2,1,0:T(8,128)(2,1)}, u32[]{:S(2)}) copy-start(bf16[8,32,1792]{2,1,0:T(8,128)(2,1)} %copy-done.1) | copy-start | bytes 2752516
  366.4 104.9 %all-gather.14.cloned.1.call-start = ((), (), s32[]{:S(2)}) async-start(), calls=%async_computation.18 | async-start | bytes 4587520 | tf_op jit(solution)/shard_map/all_gather | solution.py:66
  367.0 11.4 %all-to-all-start.3 = ((bf16[256,4,256]{0,2,1:T(8,128)(2,1)}), bf16[256,4,256]{0,2,1:T(8,128)(2,1)S(1)}, u32[]{:S(2)}, u32[]{:S(2)}) async-start(bf16[256,4,256]{0,2,1:T(8,128)(2,1)} %bitcast.6), calls=%async_computation.8 | async-start | bytes 1048576 | tf_op jit(solution)/shard_map/all_to_all | solution.py:62
  378.4 12.5 %all-to-all-start.2 = ((bf16[256,4,448]{0,2,1:T(8,128)(2,1)}), bf16[256,4,448]{0,2,1:T(8,128)(2,1)S(1)}, u32[]{:S(2)}, u32[]{:S(2)}) async-start(bf16[256,4,448]{0,2,1:T(8,128)(2,1)} %bitcast.3), calls=%async_computation.7 | async-start | bytes 1835008 | tf_op jit(solution)/shard_map/all_to_all | solution.py:61
  390.9 12.9 %all-to-all-start.1 = ((bf16[256,4,448]{0,2,1:T(8,128)(2,1)}), bf16[256,4,448]{0,2,1:T(8,128)(2,1)S(1)}, u32[]{:S(2)}, u32[]{:S(2)}) async-start(bf16[256,4,448]{0,2,1:T(8,128)(2,1)} %copy.19), calls=%async_computation.6 | async-start | bytes 1835008 | tf_op jit(solution)/shard_map/all_to_all | solution.py:60
  404.0 67.3 %copy-start.4 = (bf16[4,256,256]{2,1,0:T(8,128)(2,1)S(1)}, bf16[4,256,256]{2,1,0:T(8,128)(2,1)}, u32[]{:S(2)}) copy-start(bf16[4,256,256]{2,1,0:T(8,128)(2,1)} %copy.23) | copy-start | bytes 1572868
Sparse Core Ops, SparseCore 0:
  9.8 50.2 all-gather.5
  61.9 46.7 all-gather.7
  110.5 49.5 all-gather.9
  162.4 40.8 reduce-scatter.5
  205.7 43.1 reduce-scatter.7
  251.3 43.1 reduce-scatter.11
  296.9 37.5 all-gather.11
  337.1 45.9 reduce-scatter.9
  385.6 37.8 reduce-scatter.13
  425.2 46.0 all-gather.13
